TPU v7x, 32 devices: a whole 2x2x4 slice. The times are simulated.
32 devices in a mesh: dp: 4 (over z), expert: 4 (over y, x), tensor: 2 (over core).
Axes of the slice: x: 2, y: 2, z: 4, core: 2. Of those that a mesh axis runs over, the one named last changes fastest.
Arguments:
- hidden_in: bfloat16 [4096, 2048], P(('dp', 'expert')), may hold values from -6 to 6
- query: bfloat16 [4096, 2048], P(('dp', 'expert'), 'tensor'), may hold values from -26 to 26
- keys: bfloat16 [4096, 2048], P(('dp', 'expert'), 'tensor'), may hold values from -26 to 26
- values: bfloat16 [4096, 2048], P(('dp', 'expert'), 'tensor'), may hold values from -6 to 6
- out_proj: bfloat16 [2048, 2048], P('tensor'), may hold values from -0.125 to 0.125
- norm_gain: bfloat16 [2048], replicated, may hold values from 0.25 to 1.75
- routes: int32 [4096, 2], P(('dp', 'expert')), may hold values from 0 to 3, all different within a row; in each aligned block of 256 rows (0 to 255, 256 to 511, ...) at most 144 rows name the same one
- gates: float32 [4096, 2], P(('dp', 'expert')), may hold values from 0.2 to 1
- w_gate: bfloat16 [4, 2048, 5504], P('expert', 'dp', 'tensor'), may hold values from -0.125 to 0.125
- w_up: bfloat16 [4, 2048, 5504], P('expert', 'dp', 'tensor'), may hold values from -0.125 to 0.125
- w_down_t: bfloat16 [4, 2048, 5504], P('expert', 'dp', 'tensor'), may hold values from -0.078125 to 0.078125
Outputs:
- layer_out: bfloat16 [4096, 2048], P(('dp', 'expert'), 'tensor')
Inputs may be any that keep to these rules, and one draw needn't show every extreme that they name: `routes`: each row names 2 different experts; in the 256 rows of one block of consecutive tokens no expert is named more than 144 times, a bound that some block reaches.
All inputs are finite; a program needn't handle non-finite values.
Results may differ from a plain program's by a relative error of at most 0.0095.
Values may be sent and summed in bfloat16 or wider, within the bound.
A program may use at most 128 MiB of HBM per device.

v0:
```python
import jax
import jax.numpy as jnp
from jax import lax
from jax.sharding import PartitionSpec as P

HDIM = 128
EPSILON = 1e-05
NEGATIVE = -1e30


def slot_table(block_routes, experts, capacity):
    flat_routes = block_routes.reshape(-1)
    onehot = (flat_routes[:, None] == jnp.arange(experts, dtype=jnp.int32)[None, :]).astype(
        jnp.int32
    )
    rank_table = jnp.cumsum(onehot, axis=0) - 1
    slot_index = jnp.sum(rank_table * onehot, axis=1)
    return flat_routes * capacity + slot_index


def local(
    hidden_in, query, keys, values, out_proj, norm_gain, routes, gates, w_gate, w_up, w_down_t
):
    tok_rows, feature_width = hidden_in.shape
    head_cols = query.shape[1]
    head_count = head_cols // HDIM
    experts = lax.axis_size("expert")
    capacity = 9 * tok_rows // (4 * experts)
    tensor_count = lax.axis_size("tensor")
    slice_width = feature_width // tensor_count
    tensor_index = lax.axis_index("tensor")
    query_pos = lax.axis_index("expert") * tok_rows + jnp.arange(tok_rows, dtype=jnp.int32)
    score_scale = 1.0 / HDIM**0.5
    queries = query.astype(jnp.float32).reshape(tok_rows, head_count, HDIM)
    maxima = jnp.full((head_count, tok_rows), NEGATIVE, jnp.float32)
    key_rows = lax.all_gather(keys, "expert", axis=0, tiled=True)
    value_rows = lax.all_gather(values, "expert", axis=0, tiled=True)
    count_rows = key_rows.shape[0]
    key_pos = jnp.arange(count_rows, dtype=jnp.int32)
    key_part = key_rows.astype(jnp.float32).reshape(count_rows, head_count, HDIM)
    value_part = value_rows.astype(jnp.float32).reshape(count_rows, head_count, HDIM)
    scores = jnp.einsum("qhd,khd->hqk", queries, key_part) * score_scale
    causal = (query_pos[:, None] >= key_pos[None, :])[None]
    scores = jnp.where(causal, scores, NEGATIVE)
    new_max = jnp.maximum(maxima, jnp.max(scores, axis=-1))
    weights_now = jnp.where(causal, jnp.exp(scores - new_max[..., None]), 0.0)
    totals = jnp.sum(weights_now, axis=-1)
    weighted = jnp.einsum("hqk,khd->hqd", weights_now, value_part)
    maxima, totals, weighted = (new_max, totals, weighted)
    context = weighted / totals[..., None]
    context = jnp.transpose(context, (1, 0, 2)).reshape(tok_rows, head_cols).astype(jnp.bfloat16)
    attended = lax.psum(
        jnp.dot(context, out_proj, preferred_element_type=jnp.float32).astype(jnp.bfloat16),
        "tensor",
    ).astype(jnp.float32)
    residual = hidden_in.astype(jnp.float32) + attended
    mean_square = jnp.mean(residual * residual, axis=-1, keepdims=True)
    normed = (residual * lax.rsqrt(mean_square + EPSILON) * norm_gain.astype(jnp.float32)).astype(
        jnp.bfloat16
    )
    targets = slot_table(routes, experts, capacity)
    doubled = jnp.repeat(normed, routes.shape[1], axis=0)
    send_rows = (
        jnp.zeros((experts * capacity, feature_width), jnp.bfloat16).at[targets].set(doubled)
    )
    send_rows = send_rows.reshape(experts, capacity, feature_width)
    arrived = lax.all_to_all(send_rows, "expert", split_axis=0, concat_axis=0, tiled=True)
    slot_rows = arrived.reshape(experts * capacity, feature_width)
    gate_full, up_full, down_full = (
        lax.all_gather(w_gate, "dp", axis=1, tiled=True),
        lax.all_gather(w_up, "dp", axis=1, tiled=True),
        lax.all_gather(w_down_t, "dp", axis=1, tiled=True),
    )
    gate_out = jnp.dot(slot_rows, gate_full[0], preferred_element_type=jnp.float32)
    up_out = jnp.dot(slot_rows, up_full[0], preferred_element_type=jnp.float32)
    hidden = (jax.nn.silu(gate_out) * up_out).astype(jnp.bfloat16)
    partial_value = lax.dot_general(
        hidden, down_full[0], (((1,), (1,)), ((), ())), preferred_element_type=jnp.float32
    )
    rounded = partial_value.astype(jnp.bfloat16)
    own_slice = lax.dynamic_slice_in_dim(residual, tensor_index * slice_width, slice_width, 1)
    summed = lax.psum_scatter(
        lax.optimization_barrier(rounded).astype(jnp.float32).astype(jnp.bfloat16),
        "tensor",
        scatter_dimension=1,
        tiled=True,
    ).astype(jnp.float32)
    returned = lax.all_to_all(
        summed.reshape(experts, capacity, slice_width).astype(jnp.bfloat16),
        "expert",
        split_axis=0,
        concat_axis=0,
        tiled=True,
    ).astype(jnp.float32)
    fetched = returned.reshape(experts * capacity, slice_width)[targets].reshape(
        tok_rows, routes.shape[1], slice_width
    )
    mixture = jnp.sum(gates[:, :, None] * fetched, axis=1)
    return (own_slice + mixture).astype(jnp.bfloat16)


def solution(mesh):
    in_specs = (
        P(("dp", "expert"), None),
        P(("dp", "expert"), "tensor"),
        P(("dp", "expert"), "tensor"),
        P(("dp", "expert"), "tensor"),
        P("tensor", None),
        P(),
        P(("dp", "expert"), None),
        P(("dp", "expert"), None),
        P("expert", "dp", "tensor"),
        P("expert", "dp", "tensor"),
        P("expert", "dp", "tensor"),
    )
    out_specs = P(("dp", "expert"), "tensor")
    return jax.shard_map(local, mesh=mesh, in_specs=in_specs, out_specs=out_specs, check_vma=False)
```

profile of v0, /device:TPU:0, one launch (start us, length us, event | category | flops | bytes accessed | tf_op | source)
XLA Modules:
  0.0 761.1 jit_solution(10035004202063859870)
XLA Ops:
  10.5 37.4 %all-gather.6.cloned.1.call-done = bf16[1024,1024]{0,1:T(8,128)(2,1)} async-done(((bf16[256,1024]{0,1:T(8,128)(2,1)}), bf16[1024,1024]{0,1:T(8,128)(2,1)}) %all-gather.6.cloned.1.call-update) | async-done | bytes 2097168 | tf_op jit(solution)/shard_map/all_gather | solution.py:36
  47.9 3.4 fusion.6
  51.4 3.2 copy-done.2
  54.6 2.6 fusion.7
  57.2 27.9 %all-gather.8.cloned.1.call-done = bf16[1024,1024]{1,0:T(8,128)(2,1)} async-done(((bf16[256,1024]{1,0:T(8,128)(2,1)}), bf16[1024,1024]{1,0:T(8,128)(2,1)}) %all-gather.8.cloned.1.call-update) | async-done | bytes 2097168 | tf_op jit(solution)/shard_map/all_gather | solution.py:37
  85.1 2.9 copy.18
  88.0 5.9 divide_convert_fusion
  93.9 2.3 convolution_convert_fusion
  100.7 15.2 %all-reduce.2.cloned.1.call-done = bf16[256,2048]{1,0:T(8,128)(2,1)} async-done(((bf16[256,2048]{1,0:T(8,128)(2,1)}), bf16[256,2048]{1,0:T(8,128)(2,1)}) %all-reduce.2.cloned.1.call-update) | async-done | bytes 1048592 | tf_op jit(solution)/shard_map/psum | solution.py:52
  115.9 3.0 convert_add_fusion
  120.7 2.2 reshape.140
  122.9 5.3 scatter_custom_fusion
  128.3 32.5 %all_to_all.10 = bf16[4,144,2048]{2,1,0:T(8,128)(2,1)} all-to-all(bf16[4,144,2048]{2,1,0:T(8,128)(2,1)S(1)} %bitcast.63), channel_id=1, replica_groups=mesh['dp'=4,'expert'=4,'tensor'=2] {'expert'}, dimensions={0} | all-to-all | bytes 4718592 | tf_op jit(solution)/shard_map/all_to_all | solution.py:67
  160.7 134.2 %all-gather.10.cloned.1.call-done = bf16[1,2048,2752]{1,2,0:T(8,128)(2,1)} async-done(((bf16[1,512,2752]{1,2,0:T(8,128)(2,1)}), bf16[1,2048,2752]{1,2,0:T(8,128)(2,1)}) %all-gather.10.cloned.1.call-update) | async-done | bytes 11272208 | tf_op jit(solution)/shard_map/all_gather | solution.py:70
  294.9 13.5 %fusion.4 = f32[576,2752]{1,0:T(8,128)} fusion(bf16[576,2048]{1,0:T(8,128)(2,1)} %bitcast.64, bf16[1,2048,2752]{1,2,0:T(8,128)(2,1)} %all-gather.10.cloned.1.call-done), kind=kOutput, calls=%fused_computation.6 | convolution fusion | flops 6492782592 | bytes 19972096 | tf_op jit(solution)/shard_map/dot_general | solution.py:74
  308.4 182.9 %all-gather.12.cloned.1.call-done = bf16[1,2048,2752]{1,2,0:T(8,128)(2,1)} async-done(((bf16[1,512,2752]{1,2,0:T(8,128)(2,1)}), bf16[1,2048,2752]{1,2,0:T(8,128)(2,1)}) %all-gather.12.cloned.1.call-update) | async-done | bytes 11272208 | tf_op jit(solution)/shard_map/all_gather | solution.py:71
  491.3 196.4 %all-gather.14.cloned.1.call-done = bf16[1,2048,2752]{1,2,0:T(8,128)(2,1)} async-done(((bf16[1,512,2752]{1,2,0:T(8,128)(2,1)}), bf16[1,2048,2752]{1,2,0:T(8,128)(2,1)}) %all-gather.14.cloned.1.call-update) | async-done | bytes 11272208 | tf_op jit(solution)/shard_map/all_gather | solution.py:72
  687.6 27.1 %fusion.18 = bf16[576,2048]{1,0:T(8,128)(2,1)} fusion(bf16[1,2048,2752]{1,2,0:T(8,128)(2,1)} %all-gather.14.cloned.1.call-done, f32[576,2752]{1,0:T(8,128)} %fusion.4, bf16[576,2048]{1,0:T(8,128)(2,1)S(1)} %bitcast.65, bf16[1,2048,2752]{1,2,0:T(8,128)(2,1)} %all-gather.12.cloned.1.call-done), kind=kOutput, calls=%fused_computation.19 | convolution fusion | flops 12996255744 | bytes 33603584 | tf_op jit(solution)/shard_map/dot_general | solution.py:77
  714.7 8.2 %reduce-scatter.2.cloned.1.call-done = bf16[576,1024]{1,0:T(8,128)(2,1)} async-done(((bf16[576,2048]{1,0:T(8,128)(2,1)}), bf16[576,1024]{1,0:T(8,128)(2,1)}) %reduce-scatter.2.cloned.1.call-update) | async-done | bytes 1179664 | tf_op jit(solution)/shard_map/reduce_scatter | solution.py:82
  723.0 4.5 all-to-all-start.1
  727.7 15.7 %all-to-all-done.1 = bf16[4,144,1024]{2,1,0:T(8,128)(2,1)} async-done(((bf16[4,144,1024]{2,1,0:T(8,128)(2,1)}), bf16[4,144,1024]{2,1,0:T(8,128)(2,1)}, u32[]{:S(2)}, u32[]{:S(2)}) %all-to-all-start.1) | async-done | bytes 1179680 | tf_op jit(solution)/shard_map/all_to_all | solution.py:88
  744.9 2.7 gather_fusion
  747.6 2.5 reshape.125
  750.1 2.6 multiply_reduce_fusion
  (60 shorter events, 11.9 us)
Async XLA Ops:
  7.4 40.6 %copy-start = (bf16[256,1024]{1,0:T(8,128)(2,1)S(1)}, bf16[256,1024]{1,0:T(8,128)(2,1)}, u32[]{:S(2)}) copy-start(bf16[256,1024]{1,0:T(8,128)(2,1)} %param.12) | copy-start | bytes 1572868
  7.4 40.5 %all-gather.6.cloned.1.call-start = ((), (), s32[]{:S(2)}) async-start(), calls=%async_computation.3 | async-start | bytes 2621440 | tf_op jit(solution)/shard_map/all_gather | solution.py:36
  9.5 75.6 %all-gather.8.cloned.1.call-start = ((), (), s32[]{:S(2)}) async-start(), calls=%async_computation.4 | async-start | bytes 2621440 | tf_op jit(solution)/shard_map/all_gather | solution.py:37
  10.2 105.6 %all-reduce.2.cloned.1.call-start = ((), (), s32[]{:S(2)}) async-start(), calls=%async_computation.5 | async-start | bytes 2097152 | tf_op jit(solution)/shard_map/psum | solution.py:52
  51.3 3.2 copy-start.2
  88.0 5.9 copy-start.10
  96.1 198.8 %all-gather.10.cloned.1.call-start = ((), (), s32[]{:S(2)}) async-start(), calls=%async_computation.6 | async-start | bytes 14090240 | tf_op jit(solution)/shard_map/all_gather | solution.py:70
  96.7 1.4 copy-start.7
  96.7 1.9 copy-start.8
  96.7 19.1 %copy-start.4 = (bf16[256,2048]{1,0:T(8,128)(2,1)S(1)}, bf16[256,2048]{1,0:T(8,128)(2,1)}, u32[]{:S(2)}) copy-start(bf16[256,2048]{1,0:T(8,128)(2,1)} %param.11) | copy-start | bytes 3145732
  96.8 394.5 %all-gather.12.cloned.1.call-start = ((), (), s32[]{:S(2)}) async-start(), calls=%async_computation.7 | async-start | bytes 14090240 | tf_op jit(solution)/shard_map/all_gather | solution.py:71
  97.3 590.3 %all-gather.14.cloned.1.call-start = ((), (), s32[]{:S(2)}) async-start(), calls=%async_computation.8 | async-start | bytes 14090240 | tf_op jit(solution)/shard_map/all_gather | solution.py:72
  97.9 625.0 %reduce-scatter.2.cloned.1.call-start = ((), (), s32[]{:S(2)}) async-start(), calls=%async_computation.9 | async-start | bytes 3538944 | tf_op jit(solution)/shard_map/reduce_scatter | solution.py:82
  115.9 3.0 copy-start.5
  294.9 392.7 %copy-start.6 = (bf16[4,144,2048]{2,1,0:T(8,128)(2,1)S(1)}, bf16[4,144,2048]{2,1,0:T(8,128)(2,1)}, u32[]{:S(2)}) copy-start(bf16[4,144,2048]{2,1,0:T(8,128)(2,1)} %all_to_all.10) | copy-start | bytes 7077892
  714.7 12.8 %copy-start.9 = (f32[256,2]{0,1:T(2,128)S(1)}, f32[256,2]{0,1:T(2,128)}, u32[]{:S(2)}) copy-start(f32[256,2]{0,1:T(2,128)} %param.18) | copy-start | bytes 6148
  723.0 20.4 %all-to-all-start.1 = ((bf16[4,144,1024]{2,1,0:T(8,128)(2,1)}), bf16[4,144,1024]{2,1,0:T(8,128)(2,1)}, u32[]{:S(2)}, u32[]{:S(2)}) async-start(bf16[4,144,1024]{2,1,0:T(8,128)(2,1)} %bitcast.68), calls=%async_computation.2 | async-start | bytes 2359296 | tf_op jit(solution)/shard_map/all_to_all | solution.py:88
  747.6 6.2 copy-start.1
  750.1 2.7 copy-start.3
Sparse Core Ops, SparseCore 0:
  10.0 37.8 all-gather.5
  49.8 35.3 all-gather.7
  96.3 19.5 all-reduce.1
  714.8 8.0 reduce-scatter.1
Sparse Core Ops, SparseCore 1:
  98.3 196.6 all-gather.9
  296.4 194.8 all-gather.11
  492.8 194.8 all-gather.13
where the time goes:
time: 762 us; the launch traced here: 761 us
  waiting for transfers between devices  620 us (81%)
  matrix products  52.1 us (7%)
  blocking collectives  32.5 us (4%)
  local copies, waits for them, and re-layouts  23.4 us (3%)
  between operations  15.1 us (2%)
  other arithmetic  13 us (2%)
    all_gather x1, waiting for transfers between devices, local(): lax.all_gather(w_down_t, 'dp', axis=1, tiled=True)  196 us
    all_gather x1, waiting for transfers between devices, local(): lax.all_gather(w_up, 'dp', axis=1, tiled=True)  183 us
    all_gather x1, waiting for transfers between devices, local(): lax.all_gather(w_gate, 'dp', axis=1, tiled=True)  134 us
    all_gather x1, waiting for transfers between devices, local(): key_rows = lax.all_gather(keys, 'expert', axis=0, tiled=True)  37.4 us
    all_to_all x1, blocking collectives, local(): lax.all_to_all(send_rows, 'expert', split_axis=0, concat_axis=0, tiled=True)  32.5 us
    all_gather x1, waiting for transfers between devices, local(): value_rows = lax.all_gather(values, 'expert', axis=0, tiled=True)  27.9 us
    dot_general x1, matrix products, local(): lax.dot_general(hidden, down_full[0], (((1,), (1,)), ((), ())), preferred...  27.1 us
    all_to_all x1, waiting for transfers between devices, local(): lax.all_to_all(summed.reshape(experts, capacity, slice_width).astype(jnp....  15.7 us
  transfers between devices with their start and end apart: 8, of which 8 were waited for; matrix products, arithmetic and copies ran while one was open for 5% of the time, Pallas kernels for 0%

commit v1 on v0

--- a/solution.py
+++ b/solution.py
@@ -1,3 +1,4 @@
+import functools
 import jax
 import jax.numpy as jnp
 from jax import lax
@@ -6,6 +7,38 @@
 HDIM = 128
 EPSILON = 1e-05
 NEGATIVE = -1e30
+
+
+def perform_the_vectors(local_values, mesh_name):
+    plain, known, heard = (
+        lax.axis_size(mesh_name),
+        lax.axis_index(mesh_name),
+        local_values.shape[1],
+    )
+    arrivals = [(it, (it + 1) % plain) for it in range(plain)]
+    entries = [(it, (it - 1) % plain) for it in range(plain)]
+    finding = jnp.zeros(
+        (*local_values.shape[:1], plain * heard, *local_values.shape[2:]), local_values.dtype
+    )
+    finding = lax.dynamic_update_slice_in_dim(finding, local_values, known * heard, axis=1)
+    arr_next = b_next = local_values
+    b_now = plain // 2
+    t = 1
+    while t < b_now + 1:
+        arr_next = lax.ppermute(arr_next, axis_name=mesh_name, perm=arrivals)
+        finding = lax.dynamic_update_slice_in_dim(
+            finding, arr_next, (known - t) % plain * heard, axis=1
+        )
+        if t < plain - b_now:
+            b_next = lax.ppermute(b_next, axis_name=mesh_name, perm=entries)
+            finding = lax.dynamic_update_slice_in_dim(
+                finding, b_next, (known + t) % plain * heard, axis=1
+            )
+        t += 1
+    return finding
+
+
+solve_quarters_over_axis = functools.partial(perform_the_vectors, mesh_name="dp")
 
 
 def slot_table(block_routes, experts, capacity):
@@ -67,7 +100,7 @@
     arrived = lax.all_to_all(send_rows, "expert", split_axis=0, concat_axis=0, tiled=True)
     slot_rows = arrived.reshape(experts * capacity, feature_width)
     gate_full, up_full, down_full = (
-        lax.all_gather(w_gate, "dp", axis=1, tiled=True),
+        solve_quarters_over_axis(w_gate),
         lax.all_gather(w_up, "dp", axis=1, tiled=True),
         lax.all_gather(w_down_t, "dp", axis=1, tiled=True),
     )

time: 762 us -> 734 us (0.963)
  waiting for transfers between devices: 620 us -> 492 us
  starting transfers between devices: 4.97 us -> 116 us
  blocking collectives: 32.5 us -> 0 us
  local copies, waits for them, and re-layouts: 23.4 us -> 46.1 us
    ppermute x0 -> x3, waiting for transfers between devices: none -> 211 us  [the longest x2 198 us: perform_the_vectors(): arr_next = lax.ppermute(arr_next, axis_name=mesh_name, perm=arrivals)]
    all_gather x1, waiting for transfers between devices: 196 us -> 0.01 us  [local(): lax.all_gather(w_down_t, 'dp', axis=1, tiled=True)]
    all_gather x1 -> x0, waiting for transfers between devices: 134 us -> none  [local(): lax.all_gather(w_gate, 'dp', axis=1, tiled=True)]
    ppermute x0 -> x3, starting transfers between devices: none -> 107 us  [the longest x2 105 us: perform_the_vectors(): arr_next = lax.ppermute(arr_next, axis_name=mesh_name, perm=arrivals)]
    all_to_all x1 -> x0, blocking collectives: 32.5 us -> none  [local(): lax.all_to_all(send_rows, 'expert', split_axis=0, concat_axis=0, tiled=True)]
    psum x1, waiting for transfers between devices: 15.2 us -> 0.02 us  [local(): lax.psum(jnp.dot(context, out_proj, preferred_element_type=jnp.float32).a...]
    dynamic_update_slice x0 -> x4, local copies, waits for them, and re-layouts: none -> 15 us  [the longest x2 7.22 us: perform_the_vectors(): lax.dynamic_update_slice_in_dim(finding, arr_next, (known - t) % plain *...]
  transfers between devices with their start and end apart: 8 -> 11, of which waited for: 8 -> 8; matrix products, arithmetic and copies ran while one was open for 5% -> 8% of each run, Pallas kernels for 0% -> 0%
where the time goes in v1:
time: 734 us; the launch traced here: 733 us
  waiting for transfers between devices  492 us (67%)
  starting transfers between devices  116 us (16%)
  matrix products  50.8 us (7%)
  local copies, waits for them, and re-layouts  46.1 us (6%)
  between operations  14.9 us (2%)
  other arithmetic  13 us (2%)
    ppermute x2, waiting for transfers between devices, perform_the_vectors(): arr_next = lax.ppermute(arr_next, axis_name=mesh_name, perm=arrivals)  198 us
    all_gather x1, waiting for transfers between devices, local(): lax.all_gather(w_up, 'dp', axis=1, tiled=True)  190 us
    ppermute x2, starting transfers between devices, perform_the_vectors(): arr_next = lax.ppermute(arr_next, axis_name=mesh_name, perm=arrivals)  105 us
    all_gather x1, waiting for transfers between devices, local(): key_rows = lax.all_gather(keys, 'expert', axis=0, tiled=True)  37.4 us
    all_gather x1, waiting for transfers between devices, local(): value_rows = lax.all_gather(values, 'expert', axis=0, tiled=True)  27.9 us
    dot_general x1, matrix products, local(): lax.dot_general(hidden, down_full[0], (((1,), (1,)), ((), ())), preferred...  27.1 us
    all_to_all x1, waiting for transfers between devices, local(): lax.all_to_all(summed.reshape(experts, capacity, slice_width).astype(jnp....  15.7 us
  transfers between devices with their start and end apart: 11, of which 8 were waited for; matrix products, arithmetic and copies ran while one was open for 8% of the time, Pallas kernels for 0%

profile of v1, /device:TPU:0, one launch (start us, length us, event | category | flops | bytes accessed | tf_op | source)
XLA Modules:
  0.0 733.2 jit_solution(16798830040605215878)
XLA Ops:
  10.5 37.4 %all-gather.5.cloned.1.call-done = bf16[1024,1024]{0,1:T(8,128)(2,1)} async-done(((bf16[256,1024]{0,1:T(8,128)(2,1)}), bf16[1024,1024]{0,1:T(8,128)(2,1)}) %all-gather.5.cloned.1.call-update) | async-done | bytes 2097168 | tf_op jit(solution)/shard_map/all_gather | solution.py:69
  47.9 3.4 fusion.4
  51.4 3.2 copy-done.2
  57.2 27.9 %all-gather.7.cloned.1.call-done = bf16[1024,1024]{1,0:T(8,128)(2,1)} async-done(((bf16[256,1024]{1,0:T(8,128)(2,1)}), bf16[1024,1024]{1,0:T(8,128)(2,1)}) %all-gather.7.cloned.1.call-update) | async-done | bytes 2097168 | tf_op jit(solution)/shard_map/all_gather | solution.py:70
  85.1 2.9 copy.18
  88.0 5.9 divide_convert_fusion
  103.7 6.8 squeeze.17
  110.5 4.1 bitcast_dynamic-update-slice_fusion.3
  114.6 99.2 %collective-permute-done = bf16[1,512,2752]{1,2,0:T(8,128)(2,1)} collective-permute-done((bf16[1,512,2752]{1,2,0:T(8,128)(2,1)}, bf16[1,512,2752]{1,2,0:T(8,128)(2,1)}, u32[]{:S(2)}, u32[]{:S(2)}) %collective-permute-start) | collective-permute-done | bytes 2818080 | tf_op jit(solution)/shard_map/ppermute | solution.py:28
  213.8 103.6 %collective-permute-start.2 = (bf16[1,512,2752]{1,2,0:T(8,128)(2,1)}, bf16[1,512,2752]{1,2,0:T(8,128)(2,1)}, u32[]{:S(2)}, u32[]{:S(2)}) collective-permute-start(bf16[1,512,2752]{1,2,0:T(8,128)(2,1)} %collective-permute-done), channel_id=1, source_target_pairs={{0,8},{8,16},{16,24},{24,0},{1,9},{9,17},{17,25},{25,1},{2,10},{10... | collective-permute-start | bytes 8454152 | tf_op jit(solution)/shard_map/ppermute | solution.py:28
  317.5 3.0 convert_add_fusion
  324.5 6.3 scatter_custom_fusion
  330.8 3.6 all-to-all-start
  334.7 3.6 bitcast_dynamic-update-slice_fusion.2
  338.4 13.7 %collective-permute-done.1 = bf16[1,512,2752]{1,2,0:T(8,128)(2,1)} collective-permute-done((bf16[1,512,2752]{1,2,0:T(8,128)(2,1)}, bf16[1,512,2752]{1,2,0:T(8,128)(2,1)}, u32[]{:S(2)}, u32[]{:S(2)}) %collective-permute-start.1) | collective-permute-done | bytes 2818080 | tf_op jit(solution)/shard_map/ppermute | solution.py:33
  352.1 3.6 bitcast_dynamic-update-slice_fusion.1
  355.7 98.5 %collective-permute-done.2 = bf16[1,512,2752]{1,2,0:T(8,128)(2,1)} collective-permute-done((bf16[1,512,2752]{1,2,0:T(8,128)(2,1)}, bf16[1,512,2752]{1,2,0:T(8,128)(2,1)}, u32[]{:S(2)}, u32[]{:S(2)}) %collective-permute-start.2) | collective-permute-done | bytes 2818080 | tf_op jit(solution)/shard_map/ppermute | solution.py:28
  454.2 3.6 bitcast_dynamic-update-slice_fusion
  457.8 12.2 %fusion.33 = f32[576,2752]{1,0:T(8,128)} fusion(bf16[576,2048]{1,0:T(8,128)(2,1)S(1)} %bitcast.67, bf16[2048,2752]{0,1:T(8,128)(2,1)} %bitcast_dynamic-update-slice_fusion), kind=kOutput, calls=%fused_computation.56 | convolution fusion | flops 6492782592 | bytes 19972096 | tf_op jit(solution)/shard_map/dot_general | solution.py:107
  470.0 190.0 %all-gather.9.cloned.1.call-done = bf16[1,2048,2752]{1,2,0:T(8,128)(2,1)} async-done(((bf16[1,512,2752]{1,2,0:T(8,128)(2,1)}), bf16[1,2048,2752]{1,2,0:T(8,128)(2,1)}) %all-gather.9.cloned.1.call-update) | async-done | bytes 11272208 | tf_op jit(solution)/shard_map/all_gather | solution.py:104
  659.9 27.1 %fusion.13 = bf16[576,2048]{1,0:T(8,128)(2,1)} fusion(bf16[1,2048,2752]{1,2,0:T(8,128)(2,1)} %all-gather.11.cloned.1.call-done, f32[576,2752]{1,0:T(8,128)} %fusion.33, bf16[576,2048]{1,0:T(8,128)(2,1)S(1)} %bitcast.68, bf16[1,2048,2752]{1,2,0:T(8,128)(2,1)} %all-gather.9.cloned.1.call-done), kind=kOutput, calls=%fused_computation.18 | convolution fusion | flops 12996255744 | bytes 33603584 | tf_op jit(solution)/shard_map/dot_general | solution.py:110
  687.0 8.2 %reduce-scatter.2.cloned.1.call-done = bf16[576,1024]{1,0:T(8,128)(2,1)} async-done(((bf16[576,2048]{1,0:T(8,128)(2,1)}), bf16[576,1024]{1,0:T(8,128)(2,1)}) %reduce-scatter.2.cloned.1.call-update) | async-done | bytes 1179664 | tf_op jit(solution)/shard_map/reduce_scatter | solution.py:115
  695.2 4.5 all-to-all-start.1
  700.0 15.7 %all-to-all-done.1 = bf16[4,144,1024]{2,1,0:T(8,128)(2,1)} async-done(((bf16[4,144,1024]{2,1,0:T(8,128)(2,1)}), bf16[4,144,1024]{2,1,0:T(8,128)(2,1)}, u32[]{:S(2)}, u32[]{:S(2)}) %all-to-all-start.1) | async-done | bytes 1179680 | tf_op jit(solution)/shard_map/all_to_all | solution.py:121
  (67 shorter events, 30.4 us)
Async XLA Ops:
  7.4 40.6 %copy-start = (bf16[256,1024]{1,0:T(8,128)(2,1)S(1)}, bf16[256,1024]{1,0:T(8,128)(2,1)}, u32[]{:S(2)}) copy-start(bf16[256,1024]{1,0:T(8,128)(2,1)} %param.12) | copy-start | bytes 1572868
  7.4 40.5 %all-gather.5.cloned.1.call-start = ((), (), s32[]{:S(2)}) async-start(), calls=%async_computation.3 | async-start | bytes 2621440 | tf_op jit(solution)/shard_map/all_gather | solution.py:69
  9.5 75.6 %all-gather.7.cloned.1.call-start = ((), (), s32[]{:S(2)}) async-start(), calls=%async_computation.4 | async-start | bytes 2621440 | tf_op jit(solution)/shard_map/all_gather | solution.py:70
  10.2 307.2 %all-reduce.2.cloned.1.call-start = ((), (), s32[]{:S(2)}) async-start(), calls=%async_computation.5 | async-start | bytes 2097152 | tf_op jit(solution)/shard_map/psum | solution.py:85
  51.3 3.2 copy-start.2
  88.0 5.9 copy-start.9
  96.1 5.1 copy-start.6
  96.2 373.8 %all-gather.11.cloned.1.call-start = ((), (), s32[]{:S(2)}) async-start(), calls=%async_computation.7 | async-start | bytes 14090240 | tf_op jit(solution)/shard_map/all_gather | solution.py:105
  96.8 563.2 %all-gather.9.cloned.1.call-start = ((), (), s32[]{:S(2)}) async-start(), calls=%async_computation.6 | async-start | bytes 14090240 | tf_op jit(solution)/shard_map/all_gather | solution.py:104
  97.3 116.4 %collective-permute-start = (bf16[1,512,2752]{1,2,0:T(8,128)(2,1)}, bf16[1,512,2752]{1,2,0:T(8,128)(2,1)}, u32[]{:S(2)}, u32[]{:S(2)}) collective-permute-start(bf16[1,512,2752]{1,2,0:T(8,128)(2,1)} %param.19), channel_id=1, source_target_pairs={{0,8},{8,16},{16,24},{24,0},{1,9},{9,17},{17,25},{25,1},{2,10},{10... | collective-permute-start | bytes 8454152 | tf_op jit(solution)/shard_map/ppermute | solution.py:28
  98.9 253.2 %collective-permute-start.1 = (bf16[1,512,2752]{1,2,0:T(8,128)(2,1)}, bf16[1,512,2752]{1,2,0:T(8,128)(2,1)}, u32[]{:S(2)}, u32[]{:S(2)}) collective-permute-start(bf16[1,512,2752]{1,2,0:T(8,128)(2,1)} %param.19), channel_id=1, source_target_pairs={{0,24},{8,0},{16,8},{24,16},{1,25},{9,1},{17,9},{25,17},{2,26},{10... | collective-permute-start | bytes 8454152 | tf_op jit(solution)/shard_map/ppermute | solution.py:33
  110.5 206.9 %copy-start.7 = (bf16[2048]{0:T(1024)(128)(2,1)S(1)}, bf16[2048]{0:T(1024)(128)(2,1)}, u32[]{:S(2)}) copy-start(bf16[2048]{0:T(1024)(128)(2,1)} %param.16) | copy-start | bytes 12292
  110.5 207.0 %copy-start.4 = (bf16[256,2048]{1,0:T(8,128)(2,1)S(1)}, bf16[256,2048]{1,0:T(8,128)(2,1)}, u32[]{:S(2)}) copy-start(bf16[256,2048]{1,0:T(8,128)(2,1)} %param.11) | copy-start | bytes 3145732
  213.8 240.4 %collective-permute-start.2 = (bf16[1,512,2752]{1,2,0:T(8,128)(2,1)}, bf16[1,512,2752]{1,2,0:T(8,128)(2,1)}, u32[]{:S(2)}, u32[]{:S(2)}) collective-permute-start(bf16[1,512,2752]{1,2,0:T(8,128)(2,1)} %collective-permute-done), channel_id=1, source_target_pairs={{0,8},{8,16},{16,24},{24,0},{1,9},{9,17},{17,25},{25,1},{2,10},{10... | collective-permute-start | bytes 8454152 | tf_op jit(solution)/shard_map/ppermute | solution.py:28
  317.5 3.0 copy-start.5
  330.8 127.0 %all-to-all-start = ((bf16[4,144,2048]{2,1,0:T(8,128)(2,1)}), bf16[4,144,2048]{2,1,0:T(8,128)(2,1)S(1)}, u32[]{:S(2)}, u32[]{:S(2)}) async-start(bf16[4,144,2048]{2,1,0:T(8,128)(2,1)} %bitcast.8), calls=%async_computation | async-start | bytes 4718592 | tf_op jit(solution)/shard_map/all_to_all | solution.py:100
  334.5 360.8 %reduce-scatter.2.cloned.1.call-start = ((), (), s32[]{:S(2)}) async-start(), calls=%async_computation.8 | async-start | bytes 3538944 | tf_op jit(solution)/shard_map/reduce_scatter | solution.py:115
  687.0 12.8 %copy-start.8 = (f32[256,2]{0,1:T(2,128)S(1)}, f32[256,2]{0,1:T(2,128)}, u32[]{:S(2)}) copy-start(f32[256,2]{0,1:T(2,128)} %param.18) | copy-start | bytes 6148
  695.2 20.4 %all-to-all-start.1 = ((bf16[4,144,1024]{2,1,0:T(8,128)(2,1)}), bf16[4,144,1024]{2,1,0:T(8,128)(2,1)}, u32[]{:S(2)}, u32[]{:S(2)}) async-start(bf16[4,144,1024]{2,1,0:T(8,128)(2,1)} %bitcast.71), calls=%async_computation.2 | async-start | bytes 2359296 | tf_op jit(solution)/shard_map/all_to_all | solution.py:121
  719.9 6.2 copy-start.1
  722.4 2.7 copy-start.3
Sparse Core Ops, SparseCore 0:
  10.0 37.8 all-gather.4
  49.8 35.3 all-gather.6
  96.3 19.5 all-reduce.1
  687.1 8.0 reduce-scatter.1
Sparse Core Ops, SparseCore 1:
  98.3 366.1 all-gather.10
  466.0 193.9 all-gather.8
